TPU v7x, 32 devices: a whole 2x2x4 slice. The times are simulated.
32 devices in a mesh: section: 2 (over x), expert: 8 (over z, core), dp: 2 (over y).
Axes of the slice: x: 2, y: 2, z: 4, core: 2. Of those that a mesh axis runs over, the one named last changes fastest.
Arguments:
- fwd_input: bfloat16 [2, 768, 3584], P('section', ('expert', 'dp')), may hold values from -24 to 24
- back_saved: bfloat16 [2, 2, 768, 3584], P(None, 'section', ('expert', 'dp')), may hold values from -24 to 24
- back_grad: bfloat16 [2, 768, 3584], P('section', ('expert', 'dp')), may hold values from -6 to 6
- norm_gain: float32 [2, 3584], P('section'), may hold values from 0.3 to 3
- gate_weight: bfloat16 [2, 8, 3584, 1024], P('section', 'expert', 'dp'), may hold values from -0.09375 to 0.09375
- up_weight: bfloat16 [2, 8, 3584, 1024], P('section', 'expert', 'dp'), may hold values from -0.09375 to 0.09375
- down_weight: bfloat16 [2, 8, 1024, 3584], P('section', 'expert', None, 'dp'), may hold values from -0.1875 to 0.1875
- routes: int32 [4, 2, 768, 2], P(None, 'section', ('expert', 'dp')), may hold values from 0 to 7, as said below
- slots: int32 [4, 2, 768, 2], P(None, 'section', ('expert', 'dp')), may hold values from 0 to 12, as said below
- affinity: float32 [4, 2, 768, 2], P(None, 'section', ('expert', 'dp')), may hold values from 0.05 to 1
Outputs:
- fwd_output: bfloat16 [2, 768, 3584], P('section', ('expert', 'dp'))
- back_output: bfloat16 [2, 768, 3584], P('section', ('expert', 'dp'))
Inputs may be any that keep to these rules, and one draw needn't show every extreme that they name: A token's routes name distinct experts. In each aligned block of 48 tokens of one index of the first dimension and one section, each expert is named at most 13 times, and one expert exactly 13 times; that expert is the same for all blocks of one index of the first dimension, one section and one dp index. Within one aligned block of 48 tokens, the routes to one expert hold distinct slots.
All inputs are finite; a program needn't handle non-finite values.
Results may differ from a plain program's by a relative error of at most 0.012.
Values may be sent and summed in bfloat16 or wider, within the bound.
A program may use at most 128 MiB of HBM per device.

v0:
```python
import functools

import jax
import jax.numpy as jnp
from jax import lax
from jax.experimental import pallas as pl
from jax.experimental.pallas import tpu as pltpu
from jax.sharding import PartitionSpec as P

ROUTE_SCALE = 2.5
EPSILON = 1e-06
F32 = jnp.float32
BF16 = jnp.bfloat16
MESH = pl.DeviceIdType.MESH
TILE = 256


def swap(block):
    return lax.ppermute(block, "dp", [(0, 1), (1, 0)])


def contract_last(left, right):
    return lax.dot_general(left, right, (((1,), (1,)), ((), ())), preferred_element_type=F32)


def dot(left, right):
    return jnp.dot(left, right, preferred_element_type=F32)


def kernel(
    experts,
    sections,
    padded,
    x0_ref,
    s0_ref,
    g0_ref,
    s1_ref,
    inv_ref,
    gain_ref,
    pick_ref,
    place_ref,
    scale_ref,
    mix_ref,
    gate_ref,
    up_ref,
    down_ref,
    out_f_ref,
    out_b_ref,
    zs,
    zr,
    wide_s,
    wide_r,
    thin_s,
    thin_r,
    small_s,
    small_r,
    shift_s,
    shift_r,
    own,
    dgu,
    act,
    weighted_ref,
    z_send,
    z_recv,
    y_send,
    y_recv,
):
    section = lax.axis_index("section")
    me = lax.axis_index("expert")
    dp = lax.axis_index("dp")
    rows = experts * padded // 2
    total = experts * padded
    tokens2, half = x0_ref.shape
    tokens = tokens2 // 2
    hidden = gate_ref.shape[1]
    has_next = section < sections - 1
    has_prev = section > 0

    barrier = pltpu.get_barrier_semaphore()

    def greet(step, carry):
        pl.semaphore_signal(
            barrier, inc=1, device_id={"expert": lax.rem(me + step, experts)}, device_id_type=MESH
        )
        return carry

    lax.fori_loop(1, experts, greet, 0)
    pl.semaphore_signal(barrier, inc=1, device_id={"dp": 1 - dp}, device_id_type=MESH)

    @pl.when(has_next)
    def _():
        pl.semaphore_signal(barrier, inc=1, device_id={"section": section + 1}, device_id_type=MESH)

    @pl.when(has_prev)
    def _():
        pl.semaphore_signal(barrier, inc=1, device_id={"section": section - 1}, device_id_type=MESH)

    sides = jnp.minimum(section, 1) + jnp.minimum(sections - 1 - section, 1)
    pl.semaphore_wait(barrier, experts + sides)

    def tiles(extent, step):
        def run(j, carry):
            step(pl.ds(pl.multiple_of(j * TILE, TILE), TILE))
            return carry

        lax.fori_loop(0, extent // TILE, run, 0)

    def z_copy(a, step):
        target = lax.rem(me + step, experts)
        return pltpu.make_async_remote_copy(
            src_ref=zs.at[a, target],
            dst_ref=zr.at[a, me],
            send_sem=z_send.at[a, step],
            recv_sem=z_recv.at[a, step],
            device_id={"expert": target},
            device_id_type=MESH,
        )

    def z_start(a):
        def run(step, carry):
            z_copy(a, step).start()
            return carry

        lax.fori_loop(1, experts, run, 0)
        zr[a, pl.ds(me, 1)] = zs[a, pl.ds(me, 1)]

    def z_wait(a):
        def run(step, carry):
            z_copy(a, step).wait_recv()
            return carry

        lax.fori_loop(1, experts, run, 0)

    def z_drain(a):
        def run(step, carry):
            z_copy(a, step).wait_send()
            return carry

        lax.fori_loop(1, experts, run, 0)

    def swap_copy(src, dst, index):
        return pltpu.make_async_remote_copy(
            src_ref=src,
            dst_ref=dst,
            send_sem=y_send.at[index],
            recv_sem=y_recv.at[index],
            device_id={"dp": 1 - dp},
            device_id_type=MESH,
        )

    def wide_copy(k):
        return swap_copy(wide_s.at[k], wide_r.at[k], k)

    def thin_copy(k):
        return swap_copy(thin_s.at[k], thin_r.at[k], 6 + k)

    def small_copy(k):
        return swap_copy(small_s.at[k], small_r.at[k], 10 + k)

    def shift_copy(k, distance):
        return pltpu.make_async_remote_copy(
            src_ref=shift_s.at[k],
            dst_ref=shift_r.at[k],
            send_sem=y_send.at[13 + k],
            recv_sem=y_recv.at[13 + k],
            device_id={"section": section + distance},
            device_id_type=MESH,
        )

    def put(a, cols, values):
        zs[a, :, :, cols] = values.astype(BF16).reshape(experts, padded, TILE)

    def arrived(a):
        return zr[a].reshape(total, half)

    def arrived_cols(a, cols):
        return zr[a, :, :, cols].reshape(total, TILE)

    def split(part):
        parts = part.reshape(experts, 2, padded // 2, TILE)
        return parts[:, 0].reshape(rows, TILE), parts[:, 1].reshape(rows, TILE)

    def merge(mine, theirs):
        shape = (experts, 1, padded // 2, TILE)
        pair = [mine.astype(F32).reshape(shape), theirs.astype(F32).reshape(shape)]
        return jnp.concatenate(pair, axis=1).reshape(total, TILE).astype(BF16)

    def send_normed(x_ref, inverse, m, a):
        def step(cols):
            normed = (x_ref[:, cols].astype(F32) * inverse * gain_ref[:, cols]).astype(BF16)
            put(a, cols, dot(place_ref[m], normed))

        tiles(half, step)
        z_start(a)

    def send_grads(g_ref, m, a):
        def step(cols):
            put(a, cols, dot(place_ref[m], g_ref[:, cols]) * scale_ref[m])

        tiles(half, step)
        z_start(a)

    def gate_up(a, k):
        def step(cols):
            held = arrived(a)
            for n, w_ref in enumerate((gate_ref, up_ref)):
                mine, theirs = split(dot(held, w_ref[:, cols]))
                own[k, n, :, cols] = mine
                wide_s[k, n, :, cols] = theirs.astype(BF16)

        tiles(hidden, step)
        wide_copy(k).start()

    def active(k, t):
        wide_copy(k).wait_recv()

        def step(cols):
            gate = own[k, 0, :, cols] + wide_r[k, 0, :, cols].astype(F32)
            upper = own[k, 1, :, cols] + wide_r[k, 1, :, cols].astype(F32)
            thin_s[t, :, cols] = (gate * jax.nn.sigmoid(gate) * upper).astype(BF16)

        tiles(hidden, step)
        thin_copy(t).start()

    def down(t, a):
        thin_copy(t).wait_recv()

        def join(cols):
            act[:, cols] = merge(thin_s[t, :, cols], thin_r[t, :, cols])

        tiles(hidden, join)

        def step(cols):
            put(a, cols, dot(act[...], down_ref[:, cols]))

        tiles(half, step)
        z_start(a)

    def combine(x_ref, m, a, out_ref):
        def step(cols):
            returned = arrived_cols(a, cols)
            mixed = mix_ref[m, 0] * dot(pick_ref[m, 0], returned)
            mixed += mix_ref[m, 1] * dot(pick_ref[m, 1], returned)
            out_ref[:, cols] = (x_ref[:, cols].astype(F32) + ROUTE_SCALE * mixed).astype(BF16)

        tiles(half, step)

    def dactive(a, t):
        def step(cols):
            mine, theirs = split(contract_last(arrived(a), down_ref[cols, :]))
            own[4, 0, :, cols] = mine
            thin_s[t, :, cols] = theirs.astype(BF16)

        tiles(hidden, step)
        thin_copy(t).start()

    def dgate_up(k, t, w):
        wide_copy(k).wait_recv()
        thin_copy(t).wait_recv()

        def step(cols):
            gate = own[k, 0, :, cols] + wide_r[k, 0, :, cols].astype(F32)
            upper = own[k, 1, :, cols] + wide_r[k, 1, :, cols].astype(F32)
            dact = own[4, 0, :, cols] + thin_r[t, :, cols].astype(F32)
            sigma = jax.nn.sigmoid(gate)
            dgate = dact * upper * sigma * (1.0 + gate * (1.0 - sigma))
            wide_s[w, 0, :, cols] = dgate.astype(BF16)
            wide_s[w, 1, :, cols] = (dact * gate * sigma).astype(BF16)

        tiles(hidden, step)
        wide_copy(w).start()

    def dexpert(w, a):
        wide_copy(w).wait_recv()

        def join(cols):
            for n in range(2):
                dgu[n, :, cols] = merge(wide_s[w, n, :, cols], wide_r[w, n, :, cols])

        tiles(hidden, join)

        def step(cols):
            put(
                a,
                cols,
                contract_last(dgu[0], gate_ref[cols, :]) + contract_last(dgu[1], up_ref[cols, :]),
            )

        tiles(half, step)
        z_start(a)

    def summed(part, k):
        small_s[k] = jnp.broadcast_to(part, (tokens2, 128))
        small_copy(k).start()
        small_copy(k).wait_recv()
        theirs = small_r[k]
        both = jnp.concatenate([theirs[tokens:], theirs[:tokens]])
        return (part + both[:, :1]) / width

    width = 2 * half

    def gradient(x_ref, inverse, g_ref, m, a, k, out_ref):
        def first(j, part):
            cols = pl.ds(pl.multiple_of(j * TILE, TILE), TILE)
            returned = arrived_cols(a, cols)
            dnormed = dot(pick_ref[m, 0], returned) + dot(pick_ref[m, 1], returned)
            weighted = dnormed * gain_ref[:, cols]
            weighted_ref[:, cols] = weighted
            return part + jnp.sum(weighted * x_ref[:, cols].astype(F32), axis=-1, keepdims=True)

        part = lax.fori_loop(0, half // TILE, first, jnp.zeros((tokens2, 1), F32))
        project = summed(part, k)

        def step(cols):
            wide = x_ref[:, cols].astype(F32)
            change = inverse * (weighted_ref[:, cols] - wide * inverse * inverse * project)
            out_ref[:, cols] = (g_ref[:, cols].astype(F32) + change).astype(BF16)

        tiles(half, step)

    x1_ref, g1_ref = shift_r.at[0], shift_r.at[1]

    @pl.when(section == 0)
    def _():
        shift_r[0] = jnp.zeros((tokens2, half), BF16)

    @pl.when(section == sections - 1)
    def _():
        shift_r[1] = jnp.zeros((tokens2, half), BF16)

    send_normed(x0_ref, inv_ref[0], 0, 0)
    send_normed(s0_ref, inv_ref[1], 1, 1)
    send_grads(g0_ref, 1, 2)
    z_wait(0)
    gate_up(0, 0)
    z_wait(1)
    gate_up(1, 1)
    active(0, 0)
    down(0, 4)
    send_normed(s1_ref, inv_ref[2], 3, 3)
    z_wait(2)
    dactive(2, 1)
    dgate_up(1, 1, 4)
    dexpert(4, 5)
    z_wait(4)
    combine(x0_ref, 0, 4, shift_s.at[0])

    @pl.when(has_next)
    def _():
        shift_copy(0, 1).start()

    z_wait(3)
    gate_up(3, 3)

    @pl.when(has_prev)
    def _():
        shift_copy(0, 1).wait_recv()

    def squares(j, part):
        wide = x1_ref[:, pl.ds(pl.multiple_of(j * TILE, TILE), TILE)].astype(F32)
        return part + jnp.sum(wide * wide, axis=-1, keepdims=True)

    part = lax.fori_loop(0, half // TILE, squares, jnp.zeros((tokens2, 1), F32))
    send_normed(x1_ref, lax.rsqrt(summed(part, 0) + EPSILON), 2, 6)
    z_wait(5)
    gradient(s0_ref, inv_ref[1], g0_ref, 1, 5, 1, shift_s.at[1])

    @pl.when(has_prev)
    def _():
        shift_copy(1, -1).start()

    @pl.when(has_next)
    def _():
        shift_copy(1, -1).wait_recv()

    send_grads(g1_ref, 3, 7)
    z_wait(6)
    gate_up(6, 2)
    active(2, 2)
    down(2, 8)
    z_wait(7)
    dactive(7, 3)
    dgate_up(3, 3, 5)
    dexpert(5, 9)
    z_wait(8)
    combine(x1_ref, 2, 8, out_f_ref)
    z_wait(9)
    gradient(s1_ref, inv_ref[2], g1_ref, 3, 9, 2, out_b_ref)

    for a in range(10):
        z_drain(a)
    for k in range(6):
        wide_copy(k).wait_send()
    for k in range(4):
        thin_copy(k).wait_send()
    for k in range(3):
        small_copy(k).wait_send()

    @pl.when(has_next)
    def _():
        shift_copy(0, 1).wait_send()

    @pl.when(has_prev)
    def _():
        shift_copy(1, -1).wait_send()


def body(
    fwd_input,
    back_saved,
    back_grad,
    norm_gain,
    gate_weight,
    up_weight,
    down_weight,
    routes,
    slots,
    affinity,
):
    experts = lax.axis_size("expert")
    me = lax.axis_index("dp")
    tokens, width = fwd_input.shape[1:]
    half = width // 2
    topk = routes.shape[3]
    capacity = tokens * topk // experts + 1
    padded = -(-capacity // 8) * 16
    rows = experts * padded // 2
    gate_w, up_w, down_w = gate_weight[0, 0], up_weight[0, 0], down_weight[0, 0]
    hidden = gate_w.shape[1]

    def columns(block, index):
        return lax.dynamic_slice_in_dim(block, index * half, half, axis=-1)

    gain = columns(norm_gain[0], me)

    def both(block):
        return jnp.concatenate([columns(block, me), swap(columns(block, 1 - me))])

    def inverse_of(block):
        wide = block.astype(F32)
        return lax.rsqrt(jnp.mean(wide * wide, axis=-1) + EPSILON)

    x_first, saved_first, saved_second = fwd_input[0], back_saved[0, 0], back_saved[1, 0]
    own_mixing = affinity[:, 0] / jnp.sum(affinity[:, 0], axis=-1, keepdims=True)
    own_target = routes[:, 0] * padded + slots[:, 0]
    own_inverse = jnp.stack([inverse_of(b) for b in (x_first, saved_first, saved_second)])
    count = own_target.size
    small = jnp.concatenate(
        [own_target.astype(F32).reshape(-1), own_mixing.reshape(-1), own_inverse.reshape(-1)]
    )
    other = swap(small)
    other_target = other[:count].reshape(own_target.shape).astype(jnp.int32)
    target = jnp.concatenate([own_target, other_target + padded // 2], axis=1)
    mixing = jnp.concatenate(
        [own_mixing, other[count : 2 * count].reshape(own_mixing.shape)], axis=1
    )
    inverse = jnp.concatenate([own_inverse, other[2 * count :].reshape(own_inverse.shape)], axis=1)

    cells = jnp.arange(2 * rows, dtype=jnp.int32)
    chosen = target[:, :, :, None] == cells
    pick = jnp.swapaxes(chosen, 1, 2).astype(BF16)
    place = (
        (target[:, None, :, 0] == cells[:, None]) | (target[:, None, :, 1] == cells[:, None])
    ).astype(BF16)
    scale = jnp.sum(
        jnp.where(chosen, ROUTE_SCALE * mixing[:, :, :, None], 0.0), axis=(1, 2)
    )[:, :, None]
    mix = jnp.swapaxes(mixing, 1, 2)[:, :, :, None]
    token_pairs = 2 * tokens
    vmem = pl.BlockSpec(memory_space=pltpu.VMEM)
    sections = lax.axis_size("section")
    operands = (
        both(x_first),
        both(saved_first),
        both(back_grad[0]),
        both(saved_second),
        inverse[:, :, None],
        gain[None],
        pick,
        place,
        scale,
        mix,
        gate_w,
        up_w,
        down_w,
    )
    final_out, final_back = pl.pallas_call(
        functools.partial(kernel, experts, sections, padded),
        out_shape=[jax.ShapeDtypeStruct((token_pairs, half), BF16)] * 2,
        in_specs=[vmem] * len(operands),
        out_specs=[vmem] * 2,
        scratch_shapes=[
            pltpu.VMEM((10, experts, padded, half), BF16),
            pltpu.VMEM((10, experts, padded, half), BF16),
            pltpu.VMEM((6, 2, rows, hidden), BF16),
            pltpu.VMEM((6, 2, rows, hidden), BF16),
            pltpu.VMEM((4, rows, hidden), BF16),
            pltpu.VMEM((4, rows, hidden), BF16),
            pltpu.VMEM((3, token_pairs, 128), F32),
            pltpu.VMEM((3, token_pairs, 128), F32),
            pltpu.VMEM((2, token_pairs, half), BF16),
            pltpu.VMEM((2, token_pairs, half), BF16),
            pltpu.VMEM((5, 2, rows, hidden), F32),
            pltpu.VMEM((2, 2 * rows, hidden), BF16),
            pltpu.VMEM((2 * rows, hidden), BF16),
            pltpu.VMEM((token_pairs, half), F32),
            pltpu.SemaphoreType.DMA((10, experts)),
            pltpu.SemaphoreType.DMA((10, experts)),
            pltpu.SemaphoreType.DMA((15,)),
            pltpu.SemaphoreType.DMA((15,)),
        ],
        compiler_params=pltpu.CompilerParams(
            collective_id=0, has_side_effects=True, vmem_limit_bytes=62 * 1024 * 1024
        ),
    )(*operands)

    def whole(block):
        mine, theirs = block[:tokens], swap(block[tokens:])
        left = jnp.where(me == 0, mine, theirs)
        right = jnp.where(me == 0, theirs, mine)
        return jnp.concatenate([left, right], axis=1)[None]

    return (whole(final_out), whole(final_back))


def solution(mesh):
    placed = (
        P("section", ("expert", "dp"), None),
        P(None, "section", ("expert", "dp"), None),
        P("section", ("expert", "dp"), None),
        P("section", None),
        P("section", "expert", "dp", None),
        P("section", "expert", "dp", None),
        P("section", "expert", None, "dp"),
        P(None, "section", ("expert", "dp"), None),
        P(None, "section", ("expert", "dp"), None),
        P(None, "section", ("expert", "dp"), None),
    )
    return jax.shard_map(
        body,
        mesh=mesh,
        in_specs=placed,
        out_specs=(P("section", ("expert", "dp"), None), P("section", ("expert", "dp"), None)),
        check_vma=False,
    )
```

profile of v0, /device:TPU:20, one launch (start us, length us, event | category | flops | bytes accessed | tf_op | source)
XLA Modules:
  0.0 289.7 jit_solution(11822620055480571293)
XLA Ops:
  0.6 0.0 copy-start
  0.6 0.0 copy-start.1
  0.7 1.2 multiply_reduce_fusion.2
  1.8 1.3 multiply_reduce_fusion.1
  3.2 0.8 copy.66
  4.0 0.7 reduce_sum.48
  4.7 0.1 reshape.127
  4.8 0.7 fusion.8
  5.5 0.1 copy.65
  5.6 0.1 convert_element_type.33
  5.7 0.1 div.27.clone
  5.8 0.1 div.28
  6.0 0.1 squeeze.10
  6.2 0.6 collective-permute-start.4
  6.7 1.0 dynamic-slice_bitcast_fusion.3
  7.8 1.6 collective-permute-start.2
  9.3 1.0 dynamic-slice_bitcast_fusion.7
  10.4 0.6 collective-permute-start
  10.9 1.1 fusion.10
  12.1 1.6 collective-permute-start.3
  13.7 0.6 collective-permute-start.1
  14.3 0.0 copy-done.1
  14.3 0.0 copy-done
  14.3 0.6 constant_dynamic-slice_fusion.gain_ref
  14.9 0.0 collective-permute-done.4
  14.9 0.1 add.72
  15.1 0.1 copy.68
  15.1 0.1 pad_add_fusion
  15.2 0.1 fusion.4
  15.3 0.1 reshape.128
  15.4 0.1 maximum_bitcast_fusion.2
  15.5 0.1 concatenate.43
  15.6 0.1 copy.72
  15.7 0.1 fusion.7
  15.8 0.8 copy.75.inv_ref
  16.6 0.9 copy.77.mix_ref
  17.6 0.9 fusion.pick_ref
  18.5 0.3 select_reduce_fusion
  18.8 1.0 copy.76.scale_ref
  19.8 0.8 fusion.2.place_ref
  20.6 0.0 collective-permute-done.2
  20.6 0.8 pad_maximum_fusion.2.g0_ref
  21.3 0.0 collective-permute-done
  21.4 0.8 pad_maximum_fusion.x0_ref
  22.1 0.3 collective-permute-done.3
  22.4 0.8 pad_maximum_fusion.3.s1_ref
  23.2 1.6 collective-permute-done.1
  24.7 0.8 pad_maximum_fusion.1.s0_ref
  25.5 251.4 %shard_map.113 = (bf16[96,1792]{1,0:T(8,128)(2,1)}, bf16[96,1792]{1,0:T(8,128)(2,1)}) custom-call(bf16[96,1792]{1,0:T(8,128)(2,1)} %pad_maximum_fusion.x0_ref, bf16[96,1792]{1,0:T(8,128)(2,1)} %pad_maximum_fusion.1.s0_ref, bf16[96,1792]{1,0:T(8,128)(2,1)} %pad_maximum_fusion.2.g0_ref, bf16[96,1792]{1,0:T(8,128)(2,1)} %pad_maximum_fusion.3.s1_ref, ...), custom_call_target="tpu_custom_call" | custom-call | tf_op jit(solution)/shard_map/pallas_call | solution.py:487
  276.9 0.9 slice.51
  277.8 0.1 collective-permute-start.6
  277.9 0.9 slice.49
  278.9 2.1 collective-permute-start.5
  280.9 4.2 %collective-permute-done.6 = bf16[48,1792]{1,0:T(8,128)(2,1)S(1)} collective-permute-done((bf16[48,1792]{1,0:T(8,128)(2,1)S(1)}, bf16[48,1792]{1,0:T(8,128)(2,1)S(1)}, u32[]{:S(2)}, u32[]{:S(2)}) %collective-permute-start.6) | collective-permute-done | bytes 172064 | tf_op jit(solution)/shard_map/ppermute | solution.py:19
  285.1 0.9 broadcast_select_fusion.1
  286.1 0.8 maximum_bitcast_fusion.1
  286.8 1.2 collective-permute-done.5
  288.0 1.0 broadcast_select_fusion.3
  288.9 0.8 maximum_bitcast_fusion
  (14 shorter events, 0.1 us)
Async XLA Ops:
  0.6 13.7 %copy-start = (f32[1,3584]{1,0:T(1,128)S(1)}, f32[1,3584]{1,0:T(1,128)}, u32[]{:S(2)}) copy-start(f32[1,3584]{1,0:T(1,128)} %param.13) | copy-start | bytes 43012
  0.6 13.7 %copy-start.1 = (f32[4,1,48,2]{2,3,1,0:T(2,128)S(1)}, f32[4,1,48,2]{2,3,1,0:T(2,128)}, u32[]{:S(2)}) copy-start(f32[4,1,48,2]{2,3,1,0:T(2,128)} %param.19) | copy-start | bytes 4612
  6.2 8.7 %collective-permute-start.4 = (f32[912]{0:T(1024)S(1)}, f32[912]{0:T(1024)S(1)}, u32[]{:S(2)}, u32[]{:S(2)}) collective-permute-start(f32[912]{0:T(1024)S(1)} %pad_maximum_fusion.4), channel_id=1, source_target_pairs={{0,1},{1,0},{2,3},{3,2},{4,5},{5,4},{6,7},{7,6},{8,9},{9,8},{10,11... | collective-permute-start | bytes 10952 | tf_op jit(solution)/shard_map/ppermute | solution.py:19
  7.8 12.8 %collective-permute-start.2 = (bf16[48,1792]{1,0:T(8,128)(2,1)S(1)}, bf16[48,1792]{1,0:T(8,128)(2,1)S(1)}, u32[]{:S(2)}, u32[]{:S(2)}) collective-permute-start(bf16[48,1792]{1,0:T(8,128)(2,1)S(1)} %get-tuple-element.17), channel_id=1, source_target_pairs={{0,1},{1,0},{2,3},{3,2},{4,5},{5,4},{6,7},{7,6},{8,9},{9,8},{10,11... | collective-permute-start | bytes 516104 | tf_op jit(solution)/shard_map/ppermute | solution.py:19
  10.4 11.0 %collective-permute-start = (bf16[48,1792]{1,0:T(8,128)(2,1)S(1)}, bf16[48,1792]{1,0:T(8,128)(2,1)S(1)}, u32[]{:S(2)}, u32[]{:S(2)}) collective-permute-start(bf16[48,1792]{1,0:T(8,128)(2,1)S(1)} %get-tuple-element.21), channel_id=1, source_target_pairs={{0,1},{1,0},{2,3},{3,2},{4,5},{5,4},{6,7},{7,6},{8,9},{9,8},{10,11... | collective-permute-start | bytes 516104 | tf_op jit(solution)/shard_map/ppermute | solution.py:19
  12.1 10.3 %collective-permute-start.3 = (bf16[48,1792]{1,0:T(8,128)(2,1)S(1)}, bf16[48,1792]{1,0:T(8,128)(2,1)S(1)}, u32[]{:S(2)}, u32[]{:S(2)}) collective-permute-start(bf16[48,1792]{1,0:T(8,128)(2,1)S(1)} %get-tuple-element.15), channel_id=1, source_target_pairs={{0,1},{1,0},{2,3},{3,2},{4,5},{5,4},{6,7},{7,6},{8,9},{9,8},{10,11... | collective-permute-start | bytes 516104 | tf_op jit(solution)/shard_map/ppermute | solution.py:19
  13.7 11.0 %collective-permute-start.1 = (bf16[48,1792]{1,0:T(8,128)(2,1)S(1)}, bf16[48,1792]{1,0:T(8,128)(2,1)S(1)}, u32[]{:S(2)}, u32[]{:S(2)}) collective-permute-start(bf16[48,1792]{1,0:T(8,128)(2,1)S(1)} %get-tuple-element.19), channel_id=1, source_target_pairs={{0,1},{1,0},{2,3},{3,2},{4,5},{5,4},{6,7},{7,6},{8,9},{9,8},{10,11... | collective-permute-start | bytes 516104 | tf_op jit(solution)/shard_map/ppermute | solution.py:19
  277.8 7.3 %collective-permute-start.6 = (bf16[48,1792]{1,0:T(8,128)(2,1)S(1)}, bf16[48,1792]{1,0:T(8,128)(2,1)S(1)}, u32[]{:S(2)}, u32[]{:S(2)}) collective-permute-start(bf16[48,1792]{1,0:T(8,128)(2,1)S(1)} %slice.51), channel_id=1, source_target_pairs={{0,1},{1,0},{2,3},{3,2},{4,5},{5,4},{6,7},{7,6},{8,9},{9,8},{10,11... | collective-permute-start | bytes 516104 | tf_op jit(solution)/shard_map/ppermute | solution.py:19
  278.9 9.1 %collective-permute-start.5 = (bf16[48,1792]{1,0:T(8,128)(2,1)S(1)}, bf16[48,1792]{1,0:T(8,128)(2,1)S(1)}, u32[]{:S(2)}, u32[]{:S(2)}) collective-permute-start(bf16[48,1792]{1,0:T(8,128)(2,1)S(1)} %slice.49), channel_id=1, source_target_pairs={{0,1},{1,0},{2,3},{3,2},{4,5},{5,4},{6,7},{7,6},{8,9},{9,8},{10,11... | collective-permute-start | bytes 516104 | tf_op jit(solution)/shard_map/ppermute | solution.py:19
where the time goes:
time: 290 us
  Pallas kernels  251 us (87%)
  other arithmetic  12.7 us (4%)
  local copies, waits for them, and re-layouts  10.6 us (4%)
  waiting for transfers between devices  7.21 us (2%)
  starting transfers between devices  7.03 us (2%)
    pallas_call x1, Pallas kernels, body(): pl.pallas_call(functools.partial(kernel, experts, sections, padded), out_...  251 us
    ppermute x7, waiting for transfers between devices, swap(): return lax.ppermute(block, 'dp', [(0, 1), (1, 0)])  7.21 us
    ppermute x7, starting transfers between devices, swap(): return lax.ppermute(block, 'dp', [(0, 1), (1, 0)])  7.03 us
  transfers between devices with their start and end apart: 7, of which 4 were waited for; matrix products, arithmetic and copies ran while one was open for 5% of the time, Pallas kernels for 0%

commit v1 on v0

--- a/solution.py
+++ b/solution.py
@@ -60,6 +60,8 @@
     dgu,
     act,
     weighted_ref,
+    fin,
+    fin_r,
     z_send,
     z_recv,
     y_send,
@@ -317,6 +319,22 @@
             out_ref[:, cols] = (g_ref[:, cols].astype(F32) + change).astype(BF16)
 
         tiles(half, step)
+
+    def final_copy(k):
+        return swap_copy(fin.at[k, pl.ds(tokens, tokens)], fin_r.at[k], 15 + k)
+
+    def finish(k, out_ref):
+        final_copy(k).wait_recv()
+
+        def run(j, carry):
+            cols = pl.ds(pl.multiple_of(j * TILE, TILE), TILE)
+            mine = pl.ds(pl.multiple_of(dp * half + j * TILE, TILE), TILE)
+            theirs = pl.ds(pl.multiple_of((1 - dp) * half + j * TILE, TILE), TILE)
+            out_ref[:, mine] = fin[k, :tokens, cols]
+            out_ref[:, theirs] = fin_r[k, :, cols]
+            return carry
+
+        lax.fori_loop(0, half // TILE, run, 0)
 
     x1_ref, g1_ref = shift_r.at[0], shift_r.at[1]
 
@@ -383,9 +401,13 @@
     dgate_up(3, 3, 5)
     dexpert(5, 9)
     z_wait(8)
-    combine(x1_ref, 2, 8, out_f_ref)
+    combine(x1_ref, 2, 8, fin.at[0])
+    final_copy(0).start()
     z_wait(9)
-    gradient(s1_ref, inv_ref[2], g1_ref, 3, 9, 2, out_b_ref)
+    gradient(s1_ref, inv_ref[2], g1_ref, 3, 9, 2, fin.at[1])
+    final_copy(1).start()
+    finish(0, out_f_ref)
+    finish(1, out_b_ref)
 
     for a in range(10):
         z_drain(a)
@@ -395,6 +417,8 @@
         thin_copy(k).wait_send()
     for k in range(3):
         small_copy(k).wait_send()
+    for k in range(2):
+        final_copy(k).wait_send()
 
     @pl.when(has_next)
     def _():
@@ -486,7 +510,7 @@
     )
     final_out, final_back = pl.pallas_call(
         functools.partial(kernel, experts, sections, padded),
-        out_shape=[jax.ShapeDtypeStruct((token_pairs, half), BF16)] * 2,
+        out_shape=[jax.ShapeDtypeStruct((tokens, width), BF16)] * 2,
         in_specs=[vmem] * len(operands),
         out_specs=[vmem] * 2,
         scratch_shapes=[
@@ -504,23 +528,19 @@
             pltpu.VMEM((2, 2 * rows, hidden), BF16),
             pltpu.VMEM((2 * rows, hidden), BF16),
             pltpu.VMEM((token_pairs, half), F32),
+            pltpu.VMEM((2, token_pairs, half), BF16),
+            pltpu.VMEM((2, tokens, half), BF16),
             pltpu.SemaphoreType.DMA((10, experts)),
             pltpu.SemaphoreType.DMA((10, experts)),
-            pltpu.SemaphoreType.DMA((15,)),
-            pltpu.SemaphoreType.DMA((15,)),
+            pltpu.SemaphoreType.DMA((17,)),
+            pltpu.SemaphoreType.DMA((17,)),
         ],
         compiler_params=pltpu.CompilerParams(
             collective_id=0, has_side_effects=True, vmem_limit_bytes=62 * 1024 * 1024
         ),
     )(*operands)
 
-    def whole(block):
-        mine, theirs = block[:tokens], swap(block[tokens:])
-        left = jnp.where(me == 0, mine, theirs)
-        right = jnp.where(me == 0, theirs, mine)
-        return jnp.concatenate([left, right], axis=1)[None]
-
-    return (whole(final_out), whole(final_back))
+    return (final_out[None], final_back[None])
 
 
 def solution(mesh):

time: 290 us -> 287 us (0.990)
  waiting for transfers between devices: 7.21 us -> 1.84 us
  Pallas kernels: 251 us -> 256 us
  other arithmetic: 12.7 us -> 9.27 us
    ppermute x7 -> x5, waiting for transfers between devices: 7.21 us -> 1.84 us  [swap(): return lax.ppermute(block, 'dp', [(0, 1), (1, 0)])]
    pallas_call x1, Pallas kernels: 251 us -> 256 us  [body(): pl.pallas_call(functools.partial(kernel, experts, sections, padded), out_...]
    unnamed x5 -> x7, local copies, waits for them, and re-layouts: 0.81 us -> 4.27 us
    ppermute x7 -> x5, starting transfers between devices: 7.03 us -> 4.89 us  [swap(): return lax.ppermute(block, 'dp', [(0, 1), (1, 0)])]
  transfers between devices with their start and end apart: 7 -> 5, of which waited for: 4 -> 2; matrix products, arithmetic and copies ran while one was open for 5% -> 4% of each run, Pallas kernels for 0% -> 0%
where the time goes in v1:
time: 287 us; the launch traced here: 285 us
  Pallas kernels  256 us (89%)
  local copies, waits for them, and re-layouts  12.2 us (4%)
  other arithmetic  9.27 us (3%)
  starting transfers between devices  4.89 us (2%)
    pallas_call x1, Pallas kernels, body(): pl.pallas_call(functools.partial(kernel, experts, sections, padded), out_...  256 us
  transfers between devices with their start and end apart: 5, of which 2 were waited for; matrix products, arithmetic and copies ran while one was open for 4% of the time, Pallas kernels for 0%

profile of v1, /device:TPU:20, one launch (start us, length us, event | category | flops | bytes accessed | tf_op | source)
XLA Modules:
  0.0 284.6 jit_solution(9894674368492429249)
XLA Ops:
  0.6 0.0 copy-start
  0.6 0.0 copy-start.1
  0.7 1.2 multiply_reduce_fusion.2
  1.8 1.3 multiply_reduce_fusion.1
  3.2 0.8 copy.66
  4.0 0.7 reduce_sum.48
  4.7 0.1 reshape.127
  4.8 0.7 fusion.8
  5.5 0.1 copy.65
  5.6 0.1 convert_element_type.33
  5.7 0.1 div.27.clone
  5.8 0.1 div.28
  6.0 0.1 squeeze.10
  6.2 0.6 collective-permute-start.4
  6.7 1.0 dynamic-slice_bitcast_fusion.3
  7.8 1.6 collective-permute-start.2
  9.3 1.0 dynamic-slice_bitcast_fusion.7
  10.4 0.6 collective-permute-start
  10.9 1.1 fusion.10
  12.1 1.6 collective-permute-start.3
  13.7 0.6 collective-permute-start.1
  14.3 0.0 copy-done.1
  14.3 0.0 copy-done
  14.3 0.6 constant_dynamic-slice_fusion.gain_ref
  14.9 0.0 collective-permute-done.4
  14.9 0.1 add.72
  15.1 0.1 copy.68
  15.1 0.1 pad_add_fusion
  15.2 0.1 fusion.4
  15.3 0.1 reshape.128
  15.4 0.1 maximum_bitcast_fusion
  15.5 0.1 concatenate.37
  15.6 0.1 copy.72
  15.7 0.1 fusion.7
  15.8 0.8 copy.75.inv_ref
  16.6 1.0 copy.77.mix_ref
  17.6 0.9 fusion.pick_ref
  18.5 0.3 select_reduce_fusion
  18.8 1.0 copy.76.scale_ref
  19.8 0.8 fusion.2.place_ref
  20.6 0.0 collective-permute-done.2
  20.6 0.8 pad_maximum_fusion.2.g0_ref
  21.4 0.0 collective-permute-done
  21.4 0.8 pad_maximum_fusion.x0_ref
  22.1 0.3 collective-permute-done.3
  22.4 0.8 pad_maximum_fusion.3.s1_ref
  23.2 1.6 collective-permute-done.1
  24.7 0.8 pad_maximum_fusion.1.s0_ref
  25.5 255.7 %shard_map.113 = (bf16[48,3584]{1,0:T(8,128)(2,1)}, bf16[48,3584]{1,0:T(8,128)(2,1)}) custom-call(bf16[96,1792]{1,0:T(8,128)(2,1)} %pad_maximum_fusion.x0_ref, bf16[96,1792]{1,0:T(8,128)(2,1)} %pad_maximum_fusion.1.s0_ref, bf16[96,1792]{1,0:T(8,128)(2,1)} %pad_maximum_fusion.2.g0_ref, bf16[96,1792]{1,0:T(8,128)(2,1)} %pad_maximum_fusion.3.s1_ref, ...), custom_call_target="tpu_custom_call" | custom-call | tf_op jit(solution)/shard_map/pallas_call | solution.py:511
  281.2 1.7 copy.96
  282.9 1.7 copy.97
  (14 shorter events, 0.1 us)
Async XLA Ops:
  0.6 13.7 %copy-start = (f32[1,3584]{1,0:T(1,128)S(1)}, f32[1,3584]{1,0:T(1,128)}, u32[]{:S(2)}) copy-start(f32[1,3584]{1,0:T(1,128)} %param.13) | copy-start | bytes 43012
  0.6 13.7 %copy-start.1 = (f32[4,1,48,2]{2,3,1,0:T(2,128)S(1)}, f32[4,1,48,2]{2,3,1,0:T(2,128)}, u32[]{:S(2)}) copy-start(f32[4,1,48,2]{2,3,1,0:T(2,128)} %param.19) | copy-start | bytes 4612
  6.2 8.7 %collective-permute-start.4 = (f32[912]{0:T(1024)S(1)}, f32[912]{0:T(1024)S(1)}, u32[]{:S(2)}, u32[]{:S(2)}) collective-permute-start(f32[912]{0:T(1024)S(1)} %pad_maximum_fusion.4), channel_id=1, source_target_pairs={{0,1},{1,0},{2,3},{3,2},{4,5},{5,4},{6,7},{7,6},{8,9},{9,8},{10,11... | collective-permute-start | bytes 10952 | tf_op jit(solution)/shard_map/ppermute | solution.py:19
  7.8 12.8 %collective-permute-start.2 = (bf16[48,1792]{1,0:T(8,128)(2,1)S(1)}, bf16[48,1792]{1,0:T(8,128)(2,1)S(1)}, u32[]{:S(2)}, u32[]{:S(2)}) collective-permute-start(bf16[48,1792]{1,0:T(8,128)(2,1)S(1)} %get-tuple-element.13), channel_id=1, source_target_pairs={{0,1},{1,0},{2,3},{3,2},{4,5},{5,4},{6,7},{7,6},{8,9},{9,8},{10,11... | collective-permute-start | bytes 516104 | tf_op jit(solution)/shard_map/ppermute | solution.py:19
  10.4 11.0 %collective-permute-start = (bf16[48,1792]{1,0:T(8,128)(2,1)S(1)}, bf16[48,1792]{1,0:T(8,128)(2,1)S(1)}, u32[]{:S(2)}, u32[]{:S(2)}) collective-permute-start(bf16[48,1792]{1,0:T(8,128)(2,1)S(1)} %get-tuple-element.17), channel_id=1, source_target_pairs={{0,1},{1,0},{2,3},{3,2},{4,5},{5,4},{6,7},{7,6},{8,9},{9,8},{10,11... | collective-permute-start | bytes 516104 | tf_op jit(solution)/shard_map/ppermute | solution.py:19
  12.1 10.3 %collective-permute-start.3 = (bf16[48,1792]{1,0:T(8,128)(2,1)S(1)}, bf16[48,1792]{1,0:T(8,128)(2,1)S(1)}, u32[]{:S(2)}, u32[]{:S(2)}) collective-permute-start(bf16[48,1792]{1,0:T(8,128)(2,1)S(1)} %get-tuple-element.11), channel_id=1, source_target_pairs={{0,1},{1,0},{2,3},{3,2},{4,5},{5,4},{6,7},{7,6},{8,9},{9,8},{10,11... | collective-permute-start | bytes 516104 | tf_op jit(solution)/shard_map/ppermute | solution.py:19
  13.7 11.0 %collective-permute-start.1 = (bf16[48,1792]{1,0:T(8,128)(2,1)S(1)}, bf16[48,1792]{1,0:T(8,128)(2,1)S(1)}, u32[]{:S(2)}, u32[]{:S(2)}) collective-permute-start(bf16[48,1792]{1,0:T(8,128)(2,1)S(1)} %get-tuple-element.15), channel_id=1, source_target_pairs={{0,1},{1,0},{2,3},{3,2},{4,5},{5,4},{6,7},{7,6},{8,9},{9,8},{10,11... | collective-permute-start | bytes 516104 | tf_op jit(solution)/shard_map/ppermute | solution.py:19
